TPU v7x, 256 devices: a whole 4x4x8 slice. The times are simulated.
256 devices in a mesh: row: 16 (over y, x), col: 16 (over z, core).
Axes of the slice: x: 4, y: 4, z: 8, core: 2. Of those that a mesh axis runs over, the one named last changes fastest.
Arguments:
- a_vals: float32 [128, 64, 128, 128], P('row', 'col'), may hold values from -0.109375 to 0.109375
- a_cols: int32 [128, 64], P('row', 'col'), may hold values from 0 to 127, as said below
- a_count: int32 [128, 16], P('row', 'col'), may hold values from 0 to 4, as said below
- p_vals: float32 [128, 8, 128, 128], P('row'), may hold values from -0.75 to 0.75
- p_cols: int32 [128, 8], replicated, may hold values from 0 to 15, as said below
Outputs:
- c_out: float32 [16, 16, 128, 128], P('row', 'col')
Inputs may be any that keep to these rules, and one draw needn't show every extreme that they name: `a_cols`: the entry in slot column s lies in the fine tile columns of grid column s // 4, from (s // 4) * 8 to (s // 4 + 1) * 8 - 1. With h = i // 8: a_count[i, c] is 4 for c = h and for c = (h + 8) mod 16; between 1 and 4 for other c within cyclic distance 2 of h; 0 for all other c. With h = i // 8: p_cols[i, 0] = h, p_cols[i, 1] = (h + 8) mod 16, and every other p_cols[i, t] lies within cyclic distance 2 of h.
All inputs are finite; a program needn't handle non-finite values.
Results may differ from a plain program's by a relative error of at most 0.0003.
Values sent between devices are 32-bit elements; how exact they have to be, the bound alone decides.
A program may use at most 128 MiB of HBM per device.

v0:
```python
import jax
import jax.numpy as jnp
from jax import lax
from jax.sharding import PartitionSpec as P

highest = lax.Precision.HIGHEST


def from_root(x, axis, root):
    mine = lax.axis_index(axis) == root
    return lax.psum(jnp.where(mine, x, jnp.zeros_like(x)), axis)


def on_device(a_vals, a_cols, a_count, p_vals, p_cols):
    row_count = lax.axis_size("row")
    col_count = lax.axis_size("col")
    row_index = lax.axis_index("row")
    col_index = lax.axis_index("col")
    fine_rows, slot_count = a_cols.shape
    tile_size = a_vals.shape[-1]
    col_per_row = col_count // row_count
    block_rows = fine_rows // col_per_row
    coarse_ids = jnp.arange(col_count, dtype=jnp.int32)
    fetched = from_root(p_vals, "row", col_index // col_per_row)
    fetched_cols = lax.dynamic_slice_in_dim(p_cols, col_index * block_rows, block_rows, 0)
    fetched_hits = (fetched_cols[:, :, None] == coarse_ids[None, None, :]).astype(jnp.float32)
    live_mask = (jnp.arange(slot_count, dtype=jnp.int32)[None, :] < a_count).astype(jnp.float32)
    local_cols = a_cols - col_index * block_rows
    partial_value = jnp.zeros((col_count, fine_rows, tile_size, tile_size), jnp.float32)
    for column in range(slot_count):
        picked = jnp.take(fetched, local_cols[:, column], axis=0)
        places = jnp.take(fetched_hits, local_cols[:, column], axis=0)
        a_tiles = a_vals[:, column] * live_mask[:, column, None, None]
        products = jnp.einsum("iab,itbc->itac", a_tiles, picked, precision=highest)
        partial_value = partial_value + jnp.einsum(
            "itJ,itac->Jiac", places, products, precision=highest
        )
    ap_rows = lax.psum_scatter(partial_value, "col", scatter_dimension=0, tiled=True)[0]
    block_cols = lax.dynamic_slice_in_dim(p_cols, row_index * fine_rows, fine_rows, 0)
    block_hits = (block_cols[:, :, None] == coarse_ids[None, None, :]).astype(jnp.float32)
    spread_p = jnp.einsum("itI,itab->iIab", block_hits, p_vals, precision=highest)
    turned = lax.all_to_all(spread_p, "row", split_axis=1, concat_axis=0, tiled=True)
    c_block = jnp.einsum(
        "iIba,ibc->Iac",
        turned,
        lax.all_gather(ap_rows, "row", axis=0, tiled=True),
        precision=highest,
    )
    return c_block[:, None]


def solution(mesh):
    return jax.shard_map(
        on_device,
        mesh=mesh,
        in_specs=(
            P("row", "col", None, None),
            P("row", "col"),
            P("row", "col"),
            P("row", None, None, None),
            P(),
        ),
        out_specs=P("row", "col", None, None),
        check_vma=False,
    )
```

profile of v0, /device:TPU:1, one launch (start us, length us, event | category | flops | bytes accessed | tf_op | source)
XLA Modules:
  0.0 506.7 jit_solution(14614679422541620538)
XLA Ops:
  12.3 115.9 %all-reduce.2.cloned.1.call-done = f32[8,8,128,128]{3,2,1,0:T(8,128)} async-done(((f32[8,8,128,128]{3,2,1,0:T(8,128)}), f32[8,8,128,128]{3,2,1,0:T(8,128)}) %all-reduce.2.cloned.1.call-update) | async-done | bytes 4194320 | tf_op jit(solution)/shard_map/psum | solution.py:11
  128.2 5.0 gather_fusion.6
  133.2 9.9 %fusion.21 = f32[8,8,128,128]{2,3,1,0:T(8,128)} fusion(f32[8,8,128,128]{3,2,1,0:T(8,128)} %gather_fusion.6, pred[8]{0:T(512)(128)(4,1)S(1)} %get-tuple-element.6, f32[8,4,128,128]{3,2,1,0:T(8,128)S(1)} %copy-done.3, f32[8]{0:T(128)S(1)} %get-tuple-element.17), kind=kOutput, calls=%fused_computation.24 | convolution fusion | flops 1611792384 | bytes 8913920 | tf_op jit(solution)/shard_map/iab,itbc->itac/dot_general | solution.py:34
  143.1 5.4 %copy.27 = f32[8,8,128,128]{3,1,2,0:T(8,128)} copy(f32[8,8,128,128]{2,3,1,0:T(8,128)} %fusion.21) | data formatting | bytes 8388608 | tf_op jit(solution)/shard_map/iab,itbc->itac/transpose | solution.py:34
  148.5 5.0 gather_fusion.4
  153.5 9.9 %fusion.18 = f32[8,8,128,128]{2,3,1,0:T(8,128)} fusion(f32[8,8,128,128]{3,2,1,0:T(8,128)} %gather_fusion.4, pred[8]{0:T(512)(128)(4,1)S(1)} %get-tuple-element.21, f32[8,4,128,128]{3,2,1,0:T(8,128)S(1)} %copy-done.3, f32[8]{0:T(128)S(1)} %get-tuple-element.18), kind=kOutput, calls=%fused_computation.23 | convolution fusion | flops 1611792384 | bytes 8913920 | tf_op jit(solution)/shard_map/iab,itbc->itac/dot_general | solution.py:34
  163.4 5.4 %copy.25 = f32[8,8,128,128]{3,1,2,0:T(8,128)} copy(f32[8,8,128,128]{2,3,1,0:T(8,128)} %fusion.18) | data formatting | bytes 8388608 | tf_op jit(solution)/shard_map/iab,itbc->itac/transpose | solution.py:34
  168.8 5.0 gather_fusion.2
  173.8 9.9 %fusion.15 = f32[8,8,128,128]{2,3,1,0:T(8,128)} fusion(f32[8,8,128,128]{3,2,1,0:T(8,128)} %gather_fusion.2, pred[8]{0:T(512)(128)(4,1)S(1)} %get-tuple-element.23, f32[8,4,128,128]{3,2,1,0:T(8,128)S(1)} %copy-done.3, f32[8]{0:T(128)S(1)} %get-tuple-element.19), kind=kOutput, calls=%fused_computation.22 | convolution fusion | flops 1611792384 | bytes 8913920 | tf_op jit(solution)/shard_map/iab,itbc->itac/dot_general | solution.py:34
  183.7 5.5 %copy.23 = f32[8,8,128,128]{3,1,2,0:T(8,128)} copy(f32[8,8,128,128]{2,3,1,0:T(8,128)} %fusion.15) | data formatting | bytes 8388608 | tf_op jit(solution)/shard_map/iab,itbc->itac/transpose | solution.py:34
  189.2 4.9 gather_fusion
  194.1 9.9 %fusion.12 = f32[8,8,128,128]{2,3,1,0:T(8,128)} fusion(f32[8,8,128,128]{3,2,1,0:T(8,128)} %gather_fusion, pred[8]{0:T(512)(128)(4,1)S(1)} %get-tuple-element.25, f32[8,4,128,128]{3,2,1,0:T(8,128)S(1)} %copy-done.3, f32[8]{0:T(128)S(1)} %get-tuple-element.20), kind=kOutput, calls=%fused_computation.21 | convolution fusion | flops 1611792384 | bytes 8913920 | tf_op jit(solution)/shard_map/iab,itbc->itac/dot_general | solution.py:34
  204.0 5.3 %copy.21 = f32[8,8,128,128]{3,1,2,0:T(8,128)} copy(f32[8,8,128,128]{2,3,1,0:T(8,128)} %fusion.12) | data formatting | bytes 8388608 | tf_op jit(solution)/shard_map/iab,itbc->itac/transpose | solution.py:34
  209.4 9.4 %fusion.48 = f32[8,128,128,16]{2,3,1,0:T(8,128)S(1)} fusion(f32[8,8,128,128]{3,1,2,0:T(8,128)} %copy.25, f32[8,8,16]{2,1,0:T(8,128)S(1)} %gather_fusion.5, pred[8]{0:T(512)(128)(4,1)S(1)} %get-tuple-element.21), kind=kOutput, calls=%fused_computation.52 | convolution fusion | flops 201327616 | bytes 12587016 | tf_op jit(solution)/shard_map/itJ,itac->Jiac/dot_general | solution.py:35
  218.8 9.1 %fusion.52 = f32[8,128,128,16]{2,3,1,0:T(8,128)} fusion(f32[8,8,128,128]{3,1,2,0:T(8,128)S(1)} %copy-done.2, f32[8,8,16]{2,1,0:T(8,128)S(1)} %gather_fusion.1, pred[8]{0:T(512)(128)(4,1)S(1)} %get-tuple-element.25), kind=kOutput, calls=%fused_computation.56 | convolution fusion | flops 201327616 | bytes 12587016 | tf_op jit(solution)/shard_map/itJ,itac->Jiac/dot_general | solution.py:35
  227.9 9.2 %fusion.50 = f32[8,128,128,16]{2,3,1,0:T(8,128)} fusion(f32[8,8,128,128]{3,1,2,0:T(8,128)S(1)} %copy-done.1, f32[8,8,16]{2,1,0:T(8,128)S(1)} %gather_fusion.3, pred[8]{0:T(512)(128)(4,1)S(1)} %get-tuple-element.23), kind=kOutput, calls=%fused_computation.54 | convolution fusion | flops 201327616 | bytes 12587016 | tf_op jit(solution)/shard_map/itJ,itac->Jiac/dot_general | solution.py:35
  237.2 14.0 %add_bitcast_fusion = f32[16,8,128,128]{3,0,2,1:T(8,128)} fusion(f32[8,128,128,16]{2,3,1,0:T(8,128)S(1)} %fusion.48, f32[8,128,128,16]{2,3,1,0:T(8,128)} %fusion.52, f32[8,128,128,16]{2,3,1,0:T(8,128)} %fusion.50, f32[8,8,128,128]{3,1,2,0:T(8,128)S(1)} %copy-done, f32[8,8,16]{2,1,0:T(8,128)S(1)} %gather_fusion.7, pred[8]{0:T(512)(128)(4,1)S(1)} %get-tuple-element.6), kind=kOutput, calls=%fused_computation.10 | convolution fusion | flops 207619072 | bytes 37752840 | tf_op jit(solution)/shard_map/itJ,itac->Jiac/dot_general | solution.py:35
  251.2 9.3 %copy.28 = f32[16,8,128,128]{3,2,1,0:T(8,128)} copy(f32[16,8,128,128]{3,0,2,1:T(8,128)} %add_bitcast_fusion) | data formatting | bytes 16777216 | tf_op jit(solution)/shard_map/add | solution.py:35
  260.6 67.8 %reduce-scatter.2.cloned.1.call-done = f32[1,8,128,128]{3,2,1,0:T(8,128)} async-done(((f32[16,8,128,128]{3,2,1,0:T(8,128)}), f32[1,8,128,128]{3,2,1,0:T(8,128)}) %reduce-scatter.2.cloned.1.call-update) | async-done | bytes 524304 | tf_op jit(solution)/shard_map/reduce_scatter | solution.py:38
  328.5 8.0 %fusion.2 = f32[8,16,128,128]{3,1,2,0:T(8,128)S(1)} fusion(f32[8,8,128,128]{3,2,1,0:T(8,128)} %param.12, s32[8,8]{1,0:T(8,128)S(1)} %copy.16), kind=kOutput, calls=%fused_computation.11 | convolution fusion | flops 201327616 | bytes 12583168 | tf_op jit(solution)/shard_map/itI,itab->iIab/dot_general | solution.py:41
  336.5 2.7 copy.18
  339.2 114.6 %all_to_all.15 = f32[8,16,128,128]{3,2,0,1:T(8,128)} all-to-all(f32[8,16,128,128]{3,2,0,1:T(8,128)S(1)} %copy.18), channel_id=1, replica_groups=mesh['row'=16,'col'=16] {'row'}, dimensions={1} | all-to-all | bytes 16777216 | tf_op jit(solution)/shard_map/all_to_all | solution.py:42
  453.8 28.3 %all-gather.3.cloned.1.call-done = f32[1,128,128,128]{3,2,0,1:T(8,128)} async-done(((f32[1,8,128,128]{3,2,0,1:T(8,128)}), f32[1,128,128,128]{3,2,0,1:T(8,128)}) %all-gather.3.cloned.1.call-update) | async-done | bytes 8388624 | tf_op jit(solution)/shard_map/all_gather | solution.py:46
  482.1 17.6 %fusion.32 = f32[1,1,128,128]{3,2,1,0:T(8,128)} fusion(f32[128,128,128]{2,1,0:T(8,128)} %bitcast.116, f32[1,128,128,128]{3,2,0,1:T(8,128)} %all-gather.3.cloned.1.call-done), kind=kOutput, calls=%fused_computation.34 | convolution fusion | flops 3221225472 | bytes 16842752 | tf_op jit(solution)/shard_map/iIba,ibc->Iac/dot_general | solution.py:43
  (35 shorter events, 5.8 us)
Async XLA Ops:
  6.5 121.7 %all-reduce.2.cloned.1.call-start = ((), (), s32[]{:S(2)}) async-start(), calls=%async_computation.2 | async-start | bytes 8388608 | tf_op jit(solution)/shard_map/psum | solution.py:11
  9.0 0.7 copy-start.4
  9.1 0.8 copy-start.5
  9.1 3.2 copy-start.6
  9.1 319.3 %reduce-scatter.2.cloned.1.call-start = ((), (), s32[]{:S(2)}) async-start(), calls=%async_computation.3 | async-start | bytes 8912896 | tf_op jit(solution)/shard_map/reduce_scatter | solution.py:38
  12.3 120.9 %copy-start.3 = (f32[8,4,128,128]{3,2,1,0:T(8,128)S(1)}, f32[8,4,128,128]{3,2,1,0:T(8,128)}, u32[]{:S(2)}) copy-start(f32[8,4,128,128]{3,2,1,0:T(8,128)} %param.9) | copy-start | bytes 6291460
  209.4 9.4 %copy-start.2 = (f32[8,8,128,128]{3,1,2,0:T(8,128)S(1)}, f32[8,8,128,128]{3,1,2,0:T(8,128)}, u32[]{:S(2)}) copy-start(f32[8,8,128,128]{3,1,2,0:T(8,128)} %copy.21) | copy-start | bytes 12582916
  218.8 9.1 %copy-start.1 = (f32[8,8,128,128]{3,1,2,0:T(8,128)S(1)}, f32[8,8,128,128]{3,1,2,0:T(8,128)}, u32[]{:S(2)}) copy-start(f32[8,8,128,128]{3,1,2,0:T(8,128)} %copy.23) | copy-start | bytes 12582916
  227.9 9.2 %copy-start = (f32[8,8,128,128]{3,1,2,0:T(8,128)S(1)}, f32[8,8,128,128]{3,1,2,0:T(8,128)}, u32[]{:S(2)}) copy-start(f32[8,8,128,128]{3,1,2,0:T(8,128)} %copy.27) | copy-start | bytes 12582916
  260.5 221.5 %all-gather.3.cloned.1.call-start = ((), (), s32[]{:S(2)}) async-start(), calls=%async_computation.4 | async-start | bytes 8912896 | tf_op jit(solution)/shard_map/all_gather | solution.py:46
Sparse Core Ops, SparseCore 0:
  10.7 117.4 all-reduce.1
  260.6 67.6 reduce-scatter.1
  330.8 151.2 all-gather.2
where the time goes:
time: 516 us; the launch traced here: 507 us
  waiting for transfers between devices  212 us (41%)
  blocking collectives  115 us (22%)
  matrix products  107 us (21%)
  local copies, waits for them, and re-layouts  56.5 us (11%)
  between operations  13.7 us (3%)
    psum x1, waiting for transfers between devices, from_root(): return lax.psum(jnp.where(mine, x, jnp.zeros_like(x)), axis)  116 us
    all_to_all x1, blocking collectives, on_device(): lax.all_to_all(spread_p, 'row', split_axis=1, concat_axis=0, tiled=True)  115 us
    reduce_scatter x1, waiting for transfers between devices, on_device(): lax.psum_scatter(partial_value, 'col', scatter_dimension=0, tiled=True)[0]  67.8 us
    dot_general x4, matrix products, on_device(): jnp.einsum('itJ,itac->Jiac', places, products, precision=highest)  41.8 us
    dot_general x4, matrix products, on_device(): products = jnp.einsum('iab,itbc->itac', a_tiles, picked, precision=highest)  39.7 us
    all_gather x1, waiting for transfers between devices, on_device(): lax.all_gather(ap_rows, 'row', axis=0, tiled=True)  28.3 us
    transpose x4, local copies, waits for them, and re-layouts, on_device(): products = jnp.einsum('iab,itbc->itac', a_tiles, picked, precision=highest)  21.6 us
    gather x4, local copies, waits for them, and re-layouts, on_device(): picked = jnp.take(fetched, local_cols[:, column], axis=0)  19.8 us
  transfers between devices with their start and end apart: 3, of which 3 were waited for; matrix products, arithmetic and copies ran while one was open for 3% of the time, Pallas kernels for 0%

commit v1 on v0

v1 whole, which is shorter than its diff:
```python
import jax
import jax.numpy as jnp
from jax import lax
from jax.experimental import pallas as pl
from jax.experimental.pallas import tpu as pltpu
from jax.sharding import PartitionSpec as P

MESH = pl.DeviceIdType.MESH
N = 16
REACH = (8, 2, 14, 1, 15, 0)
PLACE = {0: 0, 1: 15, 2: 2, 3: 13, 4: 9, 6: 5, 7: 4, 8: 8, 9: 12, 10: 11, 12: 7, 13: 3, 14: 14, 15: 1}
ROWS = 8
SLOTS = 4
B = 128
K = ROWS * B


def pick(table, index):
    total = jnp.int32(0)
    for key, value in table.items():
        total = jnp.where(index == key, jnp.int32(value), total)
    return total


def among(keys, index):
    hit = index == keys[0]
    for key in keys[1:]:
        hit = jnp.logical_or(hit, index == key)
    return hit


def split(x):
    high = x.astype(jnp.bfloat16)
    return high, (x - high.astype(jnp.float32)).astype(jnp.bfloat16)


def dot3(left_high, left_low, right_high, right_low):
    total = jnp.dot(left_high, right_high, preferred_element_type=jnp.float32)
    total += jnp.dot(left_high, right_low, preferred_element_type=jnp.float32)
    return total + jnp.dot(left_low, right_high, preferred_element_type=jnp.float32)


JOBS = {place: job for job, place in PLACE.items()}
REACH_AT = {offset: at for at, offset in enumerate(REACH)}


def kernel(
    a_cols, a_count, p_cols, a_hbm, p_hbm, out,
    a_ref, p_ref, a_high, a_low, p_high, p_low, t_high, t_low,
    q_send, q_recv, c_send, c_recv, total,
    load_sem, q_send_sem, q_recv_sem, c_send_sem, c_recv_sem,
):
    row, col = lax.axis_index("row"), lax.axis_index("col")
    mine = lax.rem(col - row + N, N)
    live = among(REACH, mine)
    has_job = among(tuple(JOBS), mine)
    job = pick(JOBS, mine)
    coarse = lax.rem(row + job, N)

    load_a = pltpu.make_async_copy(a_hbm, a_ref, load_sem.at[0])
    load_p = pltpu.make_async_copy(p_hbm, p_ref, load_sem.at[1])
    load_a.start()
    load_p.start()

    def q_copy(at):
        offset = lax.rem(REACH[at] - mine + N, N)
        place = pick(PLACE, offset)
        slot = pick(REACH_AT, mine)
        target = lax.rem(col + place, N)
        own = jnp.logical_and(mine == 0, place == 0)
        copy = pltpu.make_async_remote_copy(
            src_ref=q_send.at[at], dst_ref=q_recv.at[slot],
            send_sem=q_send_sem.at[at], recv_sem=q_recv_sem.at[slot],
            device_id=(col, target), device_id_type=MESH,
        )
        return copy, own

    def q_source(at):
        used = jnp.logical_and(has_job, among(REACH, lax.rem(job + REACH[at], N)))
        source = lax.rem(row - REACH[at] + N, N)
        own = source == row if REACH[at] == 0 else jnp.bool_(False)
        own = jnp.logical_and(own, mine == 0)
        return used, own, source

    def c_copy(at):
        target = lax.rem(row + REACH[at], N)
        own = jnp.logical_and(coarse == row, target == col)
        copy = pltpu.make_async_remote_copy(
            src_ref=c_send.at[at], dst_ref=c_recv.at[at],
            send_sem=c_send_sem.at[at], recv_sem=c_recv_sem.at[at],
            device_id=(coarse, target), device_id_type=MESH,
        )
        return copy, own

    def c_source(at):
        fine = lax.rem(col - REACH[at] + N, N)
        offset = lax.rem(row - fine + N, N)
        used = among(tuple(PLACE), offset)
        place = lax.rem(fine + pick(PLACE, offset), N)
        own = jnp.logical_and(fine == row, place == col)
        return used, own, (fine, place)

    both = jnp.logical_and
    barrier = pltpu.get_barrier_semaphore()
    awaited = jnp.int32(0)
    for at in range(len(REACH)):
        used, own, source = q_source(at)

        @pl.when(both(used, ~own))
        def _():
            pl.semaphore_signal(barrier, inc=1, device_id=(source, row), device_id_type=MESH)

        used, own, source = c_source(at)

        @pl.when(both(used, ~own))
        def _():
            pl.semaphore_signal(barrier, inc=1, device_id=source, device_id_type=MESH)

        awaited += jnp.where(both(live, ~q_copy(at)[1]), 1, 0)
        awaited += jnp.where(both(has_job, ~c_copy(at)[1]), 1, 0)

    load_a.wait()

    @pl.when(live)
    def _():
        def build(i, carry):
            for k in range(ROWS):
                tile = jnp.zeros((B, B), jnp.float32)
                for s in range(SLOTS):
                    hit = jnp.logical_and(a_cols[i, s] == col * ROWS + k, s < a_count[i, 0])
                    tile += jnp.where(hit, 1.0, 0.0) * a_ref[i, s]
                high, low = split(tile)
                rows = pl.ds(pl.multiple_of(i * B, B), B)
                a_high[rows, k * B:(k + 1) * B] = high
                a_low[rows, k * B:(k + 1) * B] = low
            return carry

        lax.fori_loop(0, ROWS, build, 0)

    load_p.wait()

    @pl.when(awaited > 0)
    def _():
        pl.semaphore_wait(barrier, awaited)

    for at in range(len(REACH)):
        wanted = lax.rem(row + REACH[at], N)

        def merge(i, carry):
            tile = jnp.zeros((B, B), jnp.float32)
            for t in range(8):
                hit = p_cols[row * ROWS + i, t] == wanted
                tile += jnp.where(hit, 1.0, 0.0) * p_ref[i, t]
            rows = pl.ds(pl.multiple_of(i * B, B), B)
            high, low = split(tile)
            p_high[rows, at * B:(at + 1) * B] = high
            p_low[rows, at * B:(at + 1) * B] = low
            high, low = split(tile.T)
            t_high[:, rows] = high
            t_low[:, rows] = low
            return carry

        lax.fori_loop(0, ROWS, merge, 0)

        @pl.when(live)
        def _():
            def chunk(n, carry):
                cols = pl.ds(pl.multiple_of(n * 256, 256), 256)
                q_send[at, :, cols] = dot3(t_high[...], t_low[...], a_high[:, cols], a_low[:, cols])
                return carry

            lax.fori_loop(0, K // 256, chunk, 0)
            copy, own = q_copy(at)

            @pl.when(~own)
            def _():
                copy.start()

    @pl.when(has_job)
    def _():
        total[...] = jnp.zeros_like(total)
        for at in range(len(REACH)):
            used, own, _ = q_source(at)

            @pl.when(both(used, ~own))
            def _():
                pltpu.make_async_remote_copy(
                    src_ref=q_send.at[at], dst_ref=q_recv.at[at],
                    send_sem=q_send_sem.at[at], recv_sem=q_recv_sem.at[at],
                    device_id=(row, col), device_id_type=MESH,
                ).wait_recv()
                total[...] += q_recv[at]

            @pl.when(both(used, own))
            def _():
                total[...] += q_send[pick(REACH_AT, job)]

        high, low = split(total[...])
        for n in range(3):
            tiles = dot3(high, low, p_high[:, n * 256:(n + 1) * 256], p_low[:, n * 256:(n + 1) * 256])
            for half in range(2):
                at = 2 * n + half
                c_send[at] = tiles[:, half * B:(half + 1) * B]
                copy, own = c_copy(at)

                @pl.when(~own)
                def _():
                    copy.start()

    out[...] = jnp.zeros_like(out)
    for at in range(len(REACH)):
        used, own, _ = c_source(at)

        @pl.when(both(used, ~own))
        def _():
            pltpu.make_async_remote_copy(
                src_ref=c_send.at[at], dst_ref=c_recv.at[at],
                send_sem=c_send_sem.at[at], recv_sem=c_recv_sem.at[at],
                device_id=(row, col), device_id_type=MESH,
            ).wait_recv()
            out[0, 0] += c_recv[at]

        @pl.when(both(used, own))
        def _():
            out[0, 0] += c_send[at]

    for at in range(len(REACH)):
        copy, own = q_copy(at)

        @pl.when(both(live, ~own))
        def _():
            copy.wait_send()

        copy, own = c_copy(at)

        @pl.when(both(has_job, ~own))
        def _():
            copy.wait_send()


def on_device(a_vals, a_cols, a_count, p_vals, p_cols):
    smem = pl.BlockSpec(memory_space=pltpu.SMEM)
    hbm = pl.BlockSpec(memory_space=pl.ANY)
    spots = len(REACH)
    return pl.pallas_call(
        kernel,
        out_shape=jax.ShapeDtypeStruct((1, 1, B, B), jnp.float32),
        in_specs=[smem, smem, smem, hbm, hbm],
        out_specs=pl.BlockSpec(memory_space=pltpu.VMEM),
        scratch_shapes=[
            pltpu.VMEM((ROWS, SLOTS, B, B), jnp.float32),
            pltpu.VMEM((ROWS, 8, B, B), jnp.float32),
            pltpu.VMEM((K, K), jnp.bfloat16),
            pltpu.VMEM((K, K), jnp.bfloat16),
            pltpu.VMEM((K, spots * B), jnp.bfloat16),
            pltpu.VMEM((K, spots * B), jnp.bfloat16),
            pltpu.VMEM((B, K), jnp.bfloat16),
            pltpu.VMEM((B, K), jnp.bfloat16),
            pltpu.VMEM((spots, B, K), jnp.float32),
            pltpu.VMEM((spots, B, K), jnp.float32),
            pltpu.VMEM((spots, B, B), jnp.float32),
            pltpu.VMEM((spots, B, B), jnp.float32),
            pltpu.VMEM((B, K), jnp.float32),
            pltpu.SemaphoreType.DMA((2,)),
            pltpu.SemaphoreType.DMA((spots,)),
            pltpu.SemaphoreType.DMA((spots,)),
            pltpu.SemaphoreType.DMA((spots,)),
            pltpu.SemaphoreType.DMA((spots,)),
        ],
        compiler_params=pltpu.CompilerParams(
            collective_id=0, has_side_effects=True, vmem_limit_bytes=40 << 20
        ),
    )(a_cols, a_count, p_cols, a_vals, p_vals)


def solution(mesh):
    return jax.shard_map(
        on_device,
        mesh=mesh,
        in_specs=(
            P("row", "col", None, None),
            P("row", "col"),
            P("row", "col"),
            P("row", None, None, None),
            P(),
        ),
        out_specs=P("row", "col", None, None),
        check_vma=False,
    )
```

time: 516 us -> 74.8 us (0.14)
  the two profiles are of different devices: /device:TPU:1 before, /device:TPU:9 now
where the time goes in v1:
time: 74.8 us; the launch traced here: 74.6 us
  Pallas kernels  67.9 us (91%)
  local copies, waits for them, and re-layouts  6.68 us (9%)
    pallas_call x1, Pallas kernels, on_device(): pl.pallas_call(kernel, out_shape=jax.ShapeDtypeStruct((1, 1, B, B), jnp.f...  67.9 us
    unnamed x8, local copies, waits for them, and re-layouts  6.68 us

profile of v1, /device:TPU:9, one launch (start us, length us, event | category | flops | bytes accessed | tf_op | source)
XLA Modules:
  0.0 74.6 jit_solution(5883137806135783863)
XLA Ops:
  0.0 0.8 %copy.6.a_cols = s32[8,4]{1,0:T(8,128)S(1)} copy(s32[8,4]{0,1:T(4,128)} %param.6) | data formatting | bytes 256 | tf_op args[1]
  0.8 0.7 copy.7.a_count
  1.5 0.8 %copy.8.p_cols = s32[128,8]{1,0:T(8,128)S(1)} copy(s32[128,8]{0,1:T(8,128)} %param.9) | data formatting | bytes 8192 | tf_op args[4]
  2.3 0.0 copy-start
  2.3 2.2 %copy-done = f32[8,8,128,128]{3,2,1,0:T(8,128)S(1)} copy-done((f32[8,8,128,128]{3,2,1,0:T(8,128)S(1)}, f32[8,8,128,128]{3,2,1,0:T(8,128)}, u32[]{:S(2)}) %copy-start) | copy-done | bytes 4194328
  4.5 0.0 copy-start.1
  4.5 1.6 %copy-done.1 = f32[8,4,128,128]{3,2,1,0:T(8,128)S(1)} copy-done((f32[8,4,128,128]{3,2,1,0:T(8,128)S(1)}, f32[8,4,128,128]{3,2,1,0:T(8,128)}, u32[]{:S(2)}) %copy-start.1) | copy-done | bytes 2097176
  6.1 67.9 %shard_map.55 = f32[1,1,128,128]{3,2,1,0:T(8,128)S(1)} custom-call(s32[8,4]{1,0:T(8,128)S(1)} %copy.6.a_cols, s32[8,1]{1,0:T(8,128)S(1)} %copy.7.a_count, s32[128,8]{1,0:T(8,128)S(1)} %copy.8.p_cols, f32[8,4,128,128]{3,2,1,0:T(8,128)S(1)} %copy-done.1, f32[8,8,128,128]{3,2,1,0:T(8,128)S(1)} %copy-done), custom_call_target="tpu_custom_call" | custom-call | tf_op jit(solution)/shard_map/pallas_call | solution.py:245
  74.0 0.6 copy.10
Async XLA Ops:
  2.3 2.2 %copy-start = (f32[8,8,128,128]{3,2,1,0:T(8,128)S(1)}, f32[8,8,128,128]{3,2,1,0:T(8,128)}, u32[]{:S(2)}) copy-start(f32[8,8,128,128]{3,2,1,0:T(8,128)} %p_hbm.1) | copy-start | bytes 12582916
  4.5 1.6 %copy-start.1 = (f32[8,4,128,128]{3,2,1,0:T(8,128)S(1)}, f32[8,4,128,128]{3,2,1,0:T(8,128)}, u32[]{:S(2)}) copy-start(f32[8,4,128,128]{3,2,1,0:T(8,128)} %a_hbm.1) | copy-start | bytes 6291460

commit v2 on v1

v2 whole, which is shorter than its diff:
```python
import jax
import jax.numpy as jnp
from jax import lax
from jax.experimental import pallas as pl
from jax.experimental.pallas import tpu as pltpu
from jax.sharding import PartitionSpec as P

MESH = pl.DeviceIdType.MESH
N = 16
REACH = (8, 2, 14, 1, 15, 0)
PLACE = (
    {0: 5, 1: 60, 2: 4, 3: 0, 4: 32, 6: 8, 7: 25, 8: 56, 9: 52, 10: 44, 12: 24, 13: 9, 14: 1, 15: 61},
    {0: 1, 1: 4, 2: 61, 3: 56, 4: 36, 6: 28, 7: 24, 8: 8, 9: 52, 10: 40, 12: 16, 13: 60, 14: 0, 15: 5},
)
JOBS = 2
ROWS = 8
SLOTS = 4
B = 128
K = ROWS * B
PARTS = 4
CHUNK = 1024


def pick(table, index):
    total = jnp.int32(0)
    for key, value in table.items():
        total = jnp.where(index == key, jnp.int32(value), total)
    return total


def among(keys, index):
    hit = index == keys[0]
    for key in keys[1:]:
        hit = jnp.logical_or(hit, index == key)
    return hit


def split(x):
    high = x.astype(jnp.bfloat16)
    return high, (x - high.astype(jnp.float32)).astype(jnp.bfloat16)


def dot3(left_high, left_low, right_high, right_low):
    total = jnp.dot(left_high, right_high, preferred_element_type=jnp.float32)
    total += jnp.dot(left_high, right_low, preferred_element_type=jnp.float32)
    return total + jnp.dot(left_low, right_high, preferred_element_type=jnp.float32)


REACH_AT = {offset: at for at, offset in enumerate(REACH)}


def place_of(fine, offset):
    code = jnp.where(fine % 2 == 0, pick(PLACE[0], offset), pick(PLACE[1], offset))
    return code // 4, code % 4


def job_of(fine, place, slot):
    tables = [{code // 4: job + 1 for job, code in table.items() if code % 4 == slot} for table in PLACE]
    return jnp.where(fine % 2 == 0, pick(tables[0], place), pick(tables[1], place)) - 1


def kernel(
    a_cols, a_count, p_cols, a_hbm, p_hbm, out,
    a_ref, p_ref, a_high, a_low, p_high, p_low, sums,
    q_send, q_recv, c_send, c_recv, total,
    load_sem, q_send_sem, q_recv_sem, c_send_sem, c_recv_sem,
):
    row, col = lax.axis_index("row"), lax.axis_index("col")
    mine = lax.rem(col - row + N, N)
    live = among(REACH, mine)
    jobs = [job_of(row, mine, slot) for slot in range(JOBS)]

    load_a = pltpu.make_async_copy(a_hbm, a_ref, load_sem.at[0])
    load_p = pltpu.make_async_copy(p_hbm, p_ref, load_sem.at[1])
    load_a.start()
    load_p.start()

    def q_copy(at):
        offset = lax.rem(REACH[at] - mine + N, N)
        place, slot = place_of(col, offset)
        spot = pick(REACH_AT, mine)
        own = jnp.logical_and(mine == 0, place == 0)
        copy = pltpu.make_async_remote_copy(
            src_ref=q_send.at[at], dst_ref=q_recv.at[slot, spot],
            send_sem=q_send_sem.at[at], recv_sem=q_recv_sem.at[slot, spot],
            device_id=(col, lax.rem(col + place, N)), device_id_type=MESH,
        )
        return copy, own

    def q_source(slot, at):
        job = jobs[slot]
        used = jnp.logical_and(job >= 0, among(REACH, lax.rem(job + REACH[at], N)))
        source = lax.rem(row - REACH[at] + N, N)
        own = mine == 0 if REACH[at] == 0 else jnp.bool_(False)
        return used, own, source

    def c_copy(slot, at):
        coarse = lax.rem(row + jobs[slot] + N, N)
        target = lax.rem(row + REACH[at], N)
        own = jnp.logical_and(coarse == row, target == col)
        copy = pltpu.make_async_remote_copy(
            src_ref=c_send.at[slot, at], dst_ref=c_recv.at[at],
            send_sem=c_send_sem.at[slot, at], recv_sem=c_recv_sem.at[at],
            device_id=(coarse, target), device_id_type=MESH,
        )
        return copy, own

    def c_source(at):
        fine = lax.rem(col - REACH[at] + N, N)
        offset = lax.rem(row - fine + N, N)
        used = among(tuple(PLACE[0]), offset)
        place, slot = place_of(fine, offset)
        place = lax.rem(fine + place, N)
        own = jnp.logical_and(fine == row, place == col)
        return used, own, (fine, place), slot

    both = jnp.logical_and
    barrier = pltpu.get_barrier_semaphore()
    awaited = jnp.int32(0)
    for at in range(len(REACH)):
        used, own, source, _ = c_source(at)

        @pl.when(both(used, ~own))
        def _():
            pl.semaphore_signal(barrier, inc=1, device_id=source, device_id_type=MESH)

        awaited += jnp.where(both(live, ~q_copy(at)[1]), 1, 0)
        for slot in range(JOBS):
            used, own, source = q_source(slot, at)

            @pl.when(both(used, ~own))
            def _():
                pl.semaphore_signal(barrier, inc=1, device_id=(source, row), device_id_type=MESH)

            awaited += jnp.where(both(jobs[slot] >= 0, ~c_copy(slot, at)[1]), 1, 0)

    load_a.wait()

    @pl.when(live)
    def _():
        def build(i, carry):
            turned = [a_ref[i, s].T for s in range(SLOTS)]
            cols = pl.ds(pl.multiple_of(i * B, B), B)
            for k in range(ROWS):
                tile = jnp.zeros((B, B), jnp.float32)
                for s in range(SLOTS):
                    hit = jnp.logical_and(a_cols[s, i] == col * ROWS + k, s < a_count[0, i])
                    tile += jnp.where(hit, 1.0, 0.0) * turned[s]
                high, low = split(tile)
                a_high[k * B:(k + 1) * B, cols] = high
                a_low[k * B:(k + 1) * B, cols] = low
            return carry

        lax.fori_loop(0, ROWS, build, 0)

    load_p.wait()

    def merge(step, carry):
        i, part = step // PARTS, step % PARTS
        rows = pl.ds(pl.multiple_of(part * (B // PARTS), B // PARTS), B // PARTS)
        into = pl.ds(pl.multiple_of(step * (B // PARTS), B // PARTS), B // PARTS)
        tiles = [p_ref[i, t, rows, :] for t in range(8)]
        for at in range(len(REACH)):
            if REACH[at] == 8:
                tile = tiles[1]
            else:
                tile = tiles[0] if REACH[at] == 0 else None
                for t in range(2, 8):
                    hit = p_cols[t, row * ROWS + i] == lax.rem(row + REACH[at], N)
                    term = jnp.where(hit, 1.0, 0.0) * tiles[t]
                    tile = term if tile is None else tile + term
            high, low = split(tile)
            p_high[into, at * B:(at + 1) * B] = high
            p_low[into, at * B:(at + 1) * B] = low
        return carry

    lax.fori_loop(0, ROWS * PARTS, merge, 0)

    for pair in range(len(REACH) // 2):
        @pl.when(live)
        def _():
            cols = slice(pair * 2 * B, (pair + 1) * 2 * B)

            def chunk(n, carry):
                rows = pl.ds(pl.multiple_of(n * CHUNK, CHUNK), CHUNK)
                both_units = dot3(a_high[rows, :], a_low[rows, :], p_high[:, cols], p_low[:, cols])
                q_send[2 * pair, rows, :] = both_units[:, :B]
                q_send[2 * pair + 1, rows, :] = both_units[:, B:]
                return carry

            lax.fori_loop(0, K // CHUNK, chunk, 0)

        if pair == 0:
            @pl.when(awaited > 0)
            def _():
                pl.semaphore_wait(barrier, awaited)

        for at in (2 * pair, 2 * pair + 1):
            copy, own = q_copy(at)

            @pl.when(both(live, ~own))
            def _():
                copy.start()

    for slot in range(JOBS):
        @pl.when(jobs[slot] >= 0)
        def _():
            total[...] = jnp.zeros_like(total)
            for at in range(len(REACH)):
                used, own, _ = q_source(slot, at)

                @pl.when(both(used, ~own))
                def _():
                    pltpu.make_async_remote_copy(
                        src_ref=q_send.at[at], dst_ref=q_recv.at[slot, at],
                        send_sem=q_send_sem.at[at], recv_sem=q_recv_sem.at[slot, at],
                        device_id=(row, col), device_id_type=MESH,
                    ).wait_recv()
                    total[...] += q_recv[slot, at]

                @pl.when(both(used, own))
                def _():
                    total[...] += q_send[pick(REACH_AT, jobs[slot])]

            for k in range(ROWS):
                high, low = split(total[k * B:(k + 1) * B, :].T)
                sums[:B, k * B:(k + 1) * B] = high
                sums[B:, k * B:(k + 1) * B] = low
            for n in range(3):
                cols = slice(n * 2 * B, (n + 1) * 2 * B)
                tiles = jnp.dot(sums[...], p_high[:, cols], preferred_element_type=jnp.float32)
                tiles = tiles[:B] + tiles[B:] + jnp.dot(sums[:B, :], p_low[:, cols], preferred_element_type=jnp.float32)
                for half in range(2):
                    at = 2 * n + half
                    c_send[slot, at] = tiles[:, half * B:(half + 1) * B]
                    copy, own = c_copy(slot, at)

                    @pl.when(~own)
                    def _():
                        copy.start()

    out[...] = jnp.zeros_like(out)
    for at in range(len(REACH)):
        used, own, _, slot = c_source(at)

        @pl.when(both(used, ~own))
        def _():
            pltpu.make_async_remote_copy(
                src_ref=c_send.at[0, at], dst_ref=c_recv.at[at],
                send_sem=c_send_sem.at[0, at], recv_sem=c_recv_sem.at[at],
                device_id=(row, col), device_id_type=MESH,
            ).wait_recv()
            out[0, 0] += c_recv[at]

        @pl.when(both(used, own))
        def _():
            out[0, 0] += c_send[slot, at]

    for at in range(len(REACH)):
        copy, own = q_copy(at)

        @pl.when(both(live, ~own))
        def _():
            copy.wait_send()

        for slot in range(JOBS):
            copy, own = c_copy(slot, at)

            @pl.when(both(jobs[slot] >= 0, ~own))
            def _():
                copy.wait_send()


def on_device(a_vals, a_cols, a_count, p_vals, p_cols):
    smem = pl.BlockSpec(memory_space=pltpu.SMEM)
    hbm = pl.BlockSpec(memory_space=pl.ANY)
    spots = len(REACH)
    return pl.pallas_call(
        kernel,
        out_shape=jax.ShapeDtypeStruct((1, 1, B, B), jnp.float32),
        in_specs=[smem, smem, smem, hbm, hbm],
        out_specs=pl.BlockSpec(memory_space=pltpu.VMEM),
        scratch_shapes=[
            pltpu.VMEM((ROWS, SLOTS, B, B), jnp.float32),
            pltpu.VMEM((ROWS, 8, B, B), jnp.float32),
            pltpu.VMEM((K, K), jnp.bfloat16),
            pltpu.VMEM((K, K), jnp.bfloat16),
            pltpu.VMEM((K, spots * B), jnp.bfloat16),
            pltpu.VMEM((K, spots * B), jnp.bfloat16),
            pltpu.VMEM((2 * B, K), jnp.bfloat16),
            pltpu.VMEM((spots, K, B), jnp.float32),
            pltpu.VMEM((JOBS, spots, K, B), jnp.float32),
            pltpu.VMEM((JOBS, spots, B, B), jnp.float32),
            pltpu.VMEM((spots, B, B), jnp.float32),
            pltpu.VMEM((K, B), jnp.float32),
            pltpu.SemaphoreType.DMA((2,)),
            pltpu.SemaphoreType.DMA((spots,)),
            pltpu.SemaphoreType.DMA((JOBS, spots)),
            pltpu.SemaphoreType.DMA((JOBS, spots)),
            pltpu.SemaphoreType.DMA((spots,)),
        ],
        compiler_params=pltpu.CompilerParams(
            collective_id=0, has_side_effects=True, vmem_limit_bytes=60 << 20
        ),
    )(a_cols.T, a_count.T, p_cols.T, a_vals, p_vals)


def solution(mesh):
    return jax.shard_map(
        on_device,
        mesh=mesh,
        in_specs=(
            P("row", "col", None, None),
            P("row", "col"),
            P("row", "col"),
            P("row", None, None, None),
            P(),
        ),
        out_specs=P("row", "col", None, None),
        check_vma=False,
    )
```

time: 74.8 us -> 59.7 us (0.80)
  the two profiles are of different devices: /device:TPU:9 before, /device:TPU:210 now
where the time goes in v2:
time: 59.7 us; the launch traced here: 59.5 us
  Pallas kernels  58.1 us (97%)
  local copies, waits for them, and re-layouts  1.47 us (2%)
    pallas_call x1, Pallas kernels, on_device(): pl.pallas_call(kernel, out_shape=jax.ShapeDtypeStruct((1, 1, B, B), jnp.f...  58.1 us
    unnamed x1, local copies, waits for them, and re-layouts  1.47 us

profile of v2, /device:TPU:210, one launch (start us, length us, event | category | flops | bytes accessed | tf_op | source)
XLA Modules:
  0.0 59.5 jit_solution(10157610752378764262)
XLA Ops:
  0.0 58.1 %shard_map.55 = f32[1,1,128,128]{3,2,1,0:T(8,128)} custom-call(s32[4,8]{1,0:T(4,128)} %bitcast.4, s32[1,8]{1,0:T(1,128)} %bitcast.5, s32[8,128]{1,0:T(8,128)} %bitcast.3, f32[8,4,128,128]{3,2,1,0:T(8,128)} %a_hbm.1, f32[8,8,128,128]{3,2,1,0:T(8,128)} %p_hbm.1), custom_call_target="tpu_custom_call" | custom-call | tf_op jit(solution)/shard_map/pallas_call | solution.py:278
  58.1 1.5 %copy.7 = f32[1,1,128,128]{3,2,1,0:T(8,128)} copy(f32[1,1,128,128]{3,2,1,0:T(8,128)} %shard_map.55) | data formatting | bytes 131072

commit v3 on v2

--- a/solution.py
+++ b/solution.py
@@ -9,16 +9,21 @@
 N = 16
 REACH = (8, 2, 14, 1, 15, 0)
 PLACE = (
-    {0: 5, 1: 60, 2: 4, 3: 0, 4: 32, 6: 8, 7: 25, 8: 56, 9: 52, 10: 44, 12: 24, 13: 9, 14: 1, 15: 61},
-    {0: 1, 1: 4, 2: 61, 3: 56, 4: 36, 6: 28, 7: 24, 8: 8, 9: 52, 10: 40, 12: 16, 13: 60, 14: 0, 15: 5},
+    {0: 5, 1: 57, 2: 0, 3: 60, 4: 44, 6: 28, 7: 61, 8: 12, 9: 36, 10: 4, 12: 24, 13: 8, 14: 56, 15: 1},
+    {0: 61, 1: 1, 2: 4, 3: 56, 4: 36, 6: 60, 7: 57, 8: 8, 9: 20, 10: 40, 12: 28, 13: 9, 14: 0, 15: 5},
 )
 JOBS = 2
+ORDER = (
+    {0: 180944, 1: 181896, 2: 181896, 8: 181896, 14: 181896, 15: 181896},
+    {0: 177416, 1: 181896, 2: 181896, 8: 181896, 14: 181896, 15: 181896},
+)
 ROWS = 8
 SLOTS = 4
 B = 128
 K = ROWS * B
 PARTS = 4
-CHUNK = 1024
+PARTS_SENT = 2
+PART = K // PARTS_SENT
 
 
 def pick(table, index):
@@ -47,6 +52,7 @@
 
 
 REACH_AT = {offset: at for at, offset in enumerate(REACH)}
+RELAY = len(REACH)
 
 
 def place_of(fine, offset):
@@ -57,13 +63,18 @@
 def job_of(fine, place, slot):
     tables = [{code // 4: job + 1 for job, code in table.items() if code % 4 == slot} for table in PLACE]
     return jnp.where(fine % 2 == 0, pick(tables[0], place), pick(tables[1], place)) - 1
+
+
+def detour(row):
+    low, even = row % 4 < 2, row // 4 % 2 == 0
+    return low == even, jnp.where(low, N - 4, 4)
 
 
 def kernel(
     a_cols, a_count, p_cols, a_hbm, p_hbm, out,
     a_ref, p_ref, a_high, a_low, p_high, p_low, sums,
     q_send, q_recv, c_send, c_recv, total,
-    load_sem, q_send_sem, q_recv_sem, c_send_sem, c_recv_sem,
+    load_sem, q_send_sem, q_recv_sem, relay_sem, c_send_sem, c_recv_sem,
 ):
     row, col = lax.axis_index("row"), lax.axis_index("col")
     mine = lax.rem(col - row + N, N)
@@ -75,22 +86,48 @@
     load_a.start()
     load_p.start()
 
-    def q_copy(at):
-        offset = lax.rem(REACH[at] - mine + N, N)
+    sequence = jnp.where(col % 2 == 0, pick(ORDER[0], mine), pick(ORDER[1], mine))
+    turns = [sequence // 8**turn % 8 for turn in range(len(REACH))]
+
+    def q_copy(at, part):
+        offset = lax.rem(pick(dict(enumerate(REACH)), at) - mine + N, N)
         place, slot = place_of(col, offset)
         spot = pick(REACH_AT, mine)
         own = jnp.logical_and(mine == 0, place == 0)
+        around, step = detour(row)
+        around = jnp.logical_and(around, mine == 8)
+        spot = jnp.where(around, RELAY, spot)
+        target = jnp.where(around, lax.rem(row + step, N), col)
         copy = pltpu.make_async_remote_copy(
-            src_ref=q_send.at[at], dst_ref=q_recv.at[slot, spot],
-            send_sem=q_send_sem.at[at], recv_sem=q_recv_sem.at[slot, spot],
-            device_id=(col, lax.rem(col + place, N)), device_id_type=MESH,
+            src_ref=q_send.at[at, part], dst_ref=q_recv.at[slot, spot, part],
+            send_sem=q_send_sem.at[at, part], recv_sem=q_recv_sem.at[slot, spot, part],
+            device_id=(target, lax.rem(col + place, N)), device_id_type=MESH,
         )
         return copy, own
+
+    around, step = detour(lax.rem(row + 4, N))
+    relays = jnp.where(row % 4 < 2, around, detour(lax.rem(row + 12, N))[0])
+    onward = lax.rem(row + step, N)
+    relayed = [job_of(onward, lax.rem(col - onward + N, N), slot) for slot in range(JOBS)]
+    relayed = [
+        jnp.logical_and(relays, jnp.logical_and(job >= 0, among(REACH, lax.rem(job + 8, N)))) for job in relayed
+    ]
+
+    def relay_copy(slot, part):
+        return pltpu.make_async_remote_copy(
+            src_ref=q_recv.at[slot, RELAY, part], dst_ref=q_recv.at[slot, REACH_AT[8], part],
+            send_sem=relay_sem.at[slot, part], recv_sem=q_recv_sem.at[slot, REACH_AT[8], part],
+            device_id=(onward, col), device_id_type=MESH,
+        )
 
     def q_source(slot, at):
         job = jobs[slot]
         used = jnp.logical_and(job >= 0, among(REACH, lax.rem(job + REACH[at], N)))
-        source = lax.rem(row - REACH[at] + N, N)
+        fine = lax.rem(row - REACH[at] + N, N)
+        source = fine, row
+        if REACH[at] == 8:
+            around, step = detour(fine)
+            source = jnp.where(around, lax.rem(fine + step, N), fine), jnp.where(around, col, row)
         own = mine == 0 if REACH[at] == 0 else jnp.bool_(False)
         return used, own, source
 
@@ -124,15 +161,23 @@
         def _():
             pl.semaphore_signal(barrier, inc=1, device_id=source, device_id_type=MESH)
 
-        awaited += jnp.where(both(live, ~q_copy(at)[1]), 1, 0)
+        awaited += jnp.where(both(live, ~q_copy(at, 0)[1]), 1, 0)
         for slot in range(JOBS):
             used, own, source = q_source(slot, at)
 
             @pl.when(both(used, ~own))
             def _():
-                pl.semaphore_signal(barrier, inc=1, device_id=(source, row), device_id_type=MESH)
+                pl.semaphore_signal(barrier, inc=1, device_id=source, device_id_type=MESH)
 
             awaited += jnp.where(both(jobs[slot] >= 0, ~c_copy(slot, at)[1]), 1, 0)
+
+    origin = lax.rem(onward + 8, N)
+    for slot in range(JOBS):
+        @pl.when(relayed[slot])
+        def _():
+            pl.semaphore_signal(barrier, inc=1, device_id=(origin, onward), device_id_type=MESH)
+
+        awaited += jnp.where(relayed[slot], 1, 0)
 
     load_a.wait()
 
@@ -170,74 +215,90 @@
                     term = jnp.where(hit, 1.0, 0.0) * tiles[t]
                     tile = term if tile is None else tile + term
             high, low = split(tile)
-            p_high[into, at * B:(at + 1) * B] = high
-            p_low[into, at * B:(at + 1) * B] = low
+            p_high[at, into] = high
+            p_low[at, into] = low
         return carry
 
     lax.fori_loop(0, ROWS * PARTS, merge, 0)
 
-    for pair in range(len(REACH) // 2):
-        @pl.when(live)
-        def _():
-            cols = slice(pair * 2 * B, (pair + 1) * 2 * B)
-
-            def chunk(n, carry):
-                rows = pl.ds(pl.multiple_of(n * CHUNK, CHUNK), CHUNK)
-                both_units = dot3(a_high[rows, :], a_low[rows, :], p_high[:, cols], p_low[:, cols])
-                q_send[2 * pair, rows, :] = both_units[:, :B]
-                q_send[2 * pair + 1, rows, :] = both_units[:, B:]
-                return carry
-
-            lax.fori_loop(0, K // CHUNK, chunk, 0)
-
-        if pair == 0:
-            @pl.when(awaited > 0)
-            def _():
-                pl.semaphore_wait(barrier, awaited)
-
-        for at in (2 * pair, 2 * pair + 1):
-            copy, own = q_copy(at)
-
-            @pl.when(both(live, ~own))
-            def _():
-                copy.start()
+    def two(ref, first, second, rows=slice(None)):
+        return jnp.concatenate([ref[first, rows], ref[second, rows]], axis=1)
+
+    for part in range(PARTS_SENT):
+        for pair in range(len(REACH) // 2):
+            units = turns[2 * pair:2 * pair + 2]
+
+            @pl.when(live)
+            def _():
+                rows = slice(part * PART, (part + 1) * PART)
+                products = dot3(a_high[rows, :], a_low[rows, :], two(p_high, *units), two(p_low, *units))
+                q_send[units[0], part] = products[:, :B]
+                q_send[units[1], part] = products[:, B:]
+
+            if pair == 0 and part == 0:
+                @pl.when(awaited > 0)
+                def _():
+                    pl.semaphore_wait(barrier, awaited)
+
+            for at in units:
+                copy, own = q_copy(at, part)
+
+                @pl.when(both(live, ~own))
+                def _():
+                    copy.start()
 
     for slot in range(JOBS):
-        @pl.when(jobs[slot] >= 0)
-        def _():
-            total[...] = jnp.zeros_like(total)
-            for at in range(len(REACH)):
-                used, own, _ = q_source(slot, at)
-
-                @pl.when(both(used, ~own))
-                def _():
-                    pltpu.make_async_remote_copy(
-                        src_ref=q_send.at[at], dst_ref=q_recv.at[slot, at],
-                        send_sem=q_send_sem.at[at], recv_sem=q_recv_sem.at[slot, at],
-                        device_id=(row, col), device_id_type=MESH,
-                    ).wait_recv()
-                    total[...] += q_recv[slot, at]
-
-                @pl.when(both(used, own))
-                def _():
-                    total[...] += q_send[pick(REACH_AT, jobs[slot])]
-
-            for k in range(ROWS):
-                high, low = split(total[k * B:(k + 1) * B, :].T)
-                sums[:B, k * B:(k + 1) * B] = high
-                sums[B:, k * B:(k + 1) * B] = low
-            for n in range(3):
-                cols = slice(n * 2 * B, (n + 1) * 2 * B)
-                tiles = jnp.dot(sums[...], p_high[:, cols], preferred_element_type=jnp.float32)
-                tiles = tiles[:B] + tiles[B:] + jnp.dot(sums[:B, :], p_low[:, cols], preferred_element_type=jnp.float32)
-                for half in range(2):
-                    at = 2 * n + half
-                    c_send[slot, at] = tiles[:, half * B:(half + 1) * B]
-                    copy, own = c_copy(slot, at)
-
-                    @pl.when(~own)
+        for part in range(PARTS_SENT):
+            @pl.when(relayed[slot])
+            def _():
+                pltpu.make_async_remote_copy(
+                    src_ref=q_send.at[0, part], dst_ref=q_recv.at[slot, RELAY, part],
+                    send_sem=q_send_sem.at[0, part], recv_sem=q_recv_sem.at[slot, RELAY, part],
+                    device_id=(row, col), device_id_type=MESH,
+                ).wait_recv()
+                relay_copy(slot, part).start()
+
+    for slot in range(JOBS):
+        for part in range(PARTS_SENT):
+            @pl.when(jobs[slot] >= 0)
+            def _():
+                total[...] = jnp.zeros_like(total)
+                for at in range(len(REACH)):
+                    used, own, _ = q_source(slot, at)
+
+                    @pl.when(both(used, ~own))
                     def _():
-                        copy.start()
+                        pltpu.make_async_remote_copy(
+                            src_ref=q_send.at[at, part], dst_ref=q_recv.at[slot, at, part],
+                            send_sem=q_send_sem.at[at, part], recv_sem=q_recv_sem.at[slot, at, part],
+                            device_id=(row, col), device_id_type=MESH,
+                        ).wait_recv()
+                        total[...] += q_recv[slot, at, part]
+
+                    @pl.when(both(used, own))
+                    def _():
+                        total[...] += q_send[pick(REACH_AT, jobs[slot]), part]
+
+                for k in range(PART // B):
+                    high, low = split(total[k * B:(k + 1) * B, :].T)
+                    sums[:B, k * B:(k + 1) * B] = high
+                    sums[B:, k * B:(k + 1) * B] = low
+                rows = slice(part * PART, (part + 1) * PART)
+                for n in range(3):
+                    tiles = jnp.dot(sums[...], two(p_high, 2 * n, 2 * n + 1, rows), preferred_element_type=jnp.float32)
+                    tiles = tiles[:B] + tiles[B:] + jnp.dot(
+                        sums[:B, :], two(p_low, 2 * n, 2 * n + 1, rows), preferred_element_type=jnp.float32
+                    )
+                    for half in range(2):
+                        at = 2 * n + half
+                        tile = tiles[:, half * B:(half + 1) * B]
+                        c_send[slot, at] = tile if part == 0 else c_send[slot, at] + tile
+                        if part == PARTS_SENT - 1:
+                            copy, own = c_copy(slot, at)
+
+                            @pl.when(~own)
+                            def _():
+                                copy.start()
 
     out[...] = jnp.zeros_like(out)
     for at in range(len(REACH)):
@@ -256,13 +317,21 @@
         def _():
             out[0, 0] += c_send[slot, at]
 
+    for slot in range(JOBS):
+        for part in range(PARTS_SENT):
+            @pl.when(relayed[slot])
+            def _():
+                relay_copy(slot, part).wait_send()
+
     for at in range(len(REACH)):
-        copy, own = q_copy(at)
-
-        @pl.when(both(live, ~own))
-        def _():
-            copy.wait_send()
-
+        for part in range(PARTS_SENT):
+            copy, own = q_copy(at, part)
+
+            @pl.when(both(live, ~own))
+            def _():
+                copy.wait_send()
+
+    for at in range(len(REACH)):
         for slot in range(JOBS):
             copy, own = c_copy(slot, at)
 
@@ -285,17 +354,18 @@
             pltpu.VMEM((ROWS, 8, B, B), jnp.float32),
             pltpu.VMEM((K, K), jnp.bfloat16),
             pltpu.VMEM((K, K), jnp.bfloat16),
-            pltpu.VMEM((K, spots * B), jnp.bfloat16),
-            pltpu.VMEM((K, spots * B), jnp.bfloat16),
-            pltpu.VMEM((2 * B, K), jnp.bfloat16),
-            pltpu.VMEM((spots, K, B), jnp.float32),
-            pltpu.VMEM((JOBS, spots, K, B), jnp.float32),
+            pltpu.VMEM((spots, K, B), jnp.bfloat16),
+            pltpu.VMEM((spots, K, B), jnp.bfloat16),
+            pltpu.VMEM((2 * B, PART), jnp.bfloat16),
+            pltpu.VMEM((spots, PARTS_SENT, PART, B), jnp.float32),
+            pltpu.VMEM((JOBS, spots + 1, PARTS_SENT, PART, B), jnp.float32),
             pltpu.VMEM((JOBS, spots, B, B), jnp.float32),
             pltpu.VMEM((spots, B, B), jnp.float32),
-            pltpu.VMEM((K, B), jnp.float32),
+            pltpu.VMEM((PART, B), jnp.float32),
             pltpu.SemaphoreType.DMA((2,)),
-            pltpu.SemaphoreType.DMA((spots,)),
-            pltpu.SemaphoreType.DMA((JOBS, spots)),
+            pltpu.SemaphoreType.DMA((spots, PARTS_SENT)),
+            pltpu.SemaphoreType.DMA((JOBS, spots + 1, PARTS_SENT)),
+            pltpu.SemaphoreType.DMA((JOBS, PARTS_SENT)),
             pltpu.SemaphoreType.DMA((JOBS, spots)),
             pltpu.SemaphoreType.DMA((spots,)),
         ],

time: 59.7 us -> 54.4 us (0.911)
  the two profiles are of different devices: /device:TPU:210 before, /device:TPU:1 now
where the time goes in v3:
time: 54.4 us; the launch traced here: 53.9 us
  Pallas kernels  52.5 us (97%)
  local copies, waits for them, and re-layouts  1.47 us (3%)
    pallas_call x1, Pallas kernels, on_device(): pl.pallas_call(kernel, out_shape=jax.ShapeDtypeStruct((1, 1, B, B), jnp.f...  52.5 us
    unnamed x1, local copies, waits for them, and re-layouts  1.47 us

profile of v3, /device:TPU:1, one launch (start us, length us, event | category | flops | bytes accessed | tf_op | source)
XLA Modules:
  0.0 53.9 jit_solution(16794741167191117013)
XLA Ops:
  0.0 52.5 %shard_map.55 = f32[1,1,128,128]{3,2,1,0:T(8,128)} custom-call(s32[4,8]{1,0:T(4,128)} %bitcast.4, s32[1,8]{1,0:T(1,128)} %bitcast.5, s32[8,128]{1,0:T(8,128)} %bitcast.3, f32[8,4,128,128]{3,2,1,0:T(8,128)} %a_hbm.1, f32[8,8,128,128]{3,2,1,0:T(8,128)} %p_hbm.1), custom_call_target="tpu_custom_call" | custom-call | tf_op jit(solution)/shard_map/pallas_call | solution.py:347
  52.5 1.5 %copy.7 = f32[1,1,128,128]{3,2,1,0:T(8,128)} copy(f32[1,1,128,128]{3,2,1,0:T(8,128)} %shard_map.55) | data formatting | bytes 131072

commit v4 on v3

--- a/solution.py
+++ b/solution.py
@@ -7,7 +7,7 @@
 
 MESH = pl.DeviceIdType.MESH
 N = 16
-REACH = (8, 2, 14, 1, 15, 0)
+REACH = (8, 14, 2, 15, 1, 0)
 PLACE = (
     {0: 5, 1: 57, 2: 0, 3: 60, 4: 44, 6: 28, 7: 61, 8: 12, 9: 36, 10: 4, 12: 24, 13: 8, 14: 56, 15: 1},
     {0: 61, 1: 1, 2: 4, 3: 56, 4: 36, 6: 60, 7: 57, 8: 8, 9: 20, 10: 40, 12: 28, 13: 9, 14: 0, 15: 5},
@@ -235,7 +235,11 @@
                 q_send[units[0], part] = products[:, :B]
                 q_send[units[1], part] = products[:, B:]
 
-            if pair == 0 and part == 0:
+            if part == 0 and pair == 0:
+                continue
+            if part == 0 and pair == 1:
+                units = turns[:4]
+
                 @pl.when(awaited > 0)
                 def _():
                     pl.semaphore_wait(barrier, awaited)
@@ -258,8 +262,8 @@
                 ).wait_recv()
                 relay_copy(slot, part).start()
 
-    for slot in range(JOBS):
-        for part in range(PARTS_SENT):
+    for part in range(PARTS_SENT):
+        for slot in range(JOBS):
             @pl.when(jobs[slot] >= 0)
             def _():
                 total[...] = jnp.zeros_like(total)

time: 54.4 us -> 55.5 us (1.020)
  the two profiles are of different devices: /device:TPU:1 before, /device:TPU:90 now
where the time goes in v4:
time: 55.5 us; the launch traced here: 55.3 us
  Pallas kernels  53.8 us (97%)
  local copies, waits for them, and re-layouts  1.47 us (3%)
    pallas_call x1, Pallas kernels, on_device(): pl.pallas_call(kernel, out_shape=jax.ShapeDtypeStruct((1, 1, B, B), jnp.f...  53.8 us
    unnamed x1, local copies, waits for them, and re-layouts  1.47 us

profile of v4, /device:TPU:90, one launch (start us, length us, event | category | flops | bytes accessed | tf_op | source)
XLA Modules:
  0.0 55.3 jit_solution(5053941270922034995)
XLA Ops:
  0.0 53.8 %shard_map.55 = f32[1,1,128,128]{3,2,1,0:T(8,128)} custom-call(s32[4,8]{1,0:T(4,128)} %bitcast.4, s32[1,8]{1,0:T(1,128)} %bitcast.5, s32[8,128]{1,0:T(8,128)} %bitcast.3, f32[8,4,128,128]{3,2,1,0:T(8,128)} %a_hbm.1, f32[8,8,128,128]{3,2,1,0:T(8,128)} %p_hbm.1), custom_call_target="tpu_custom_call" | custom-call | tf_op jit(solution)/shard_map/pallas_call | solution.py:351
  53.9 1.5 %copy.7 = f32[1,1,128,128]{3,2,1,0:T(8,128)} copy(f32[1,1,128,128]{3,2,1,0:T(8,128)} %shard_map.55) | data formatting | bytes 131072
